TPU v7x, 32 devices: a whole 2x2x4 slice. The times are simulated.
32 devices in a mesh: dp: 2 (over y), shard: 16 (over z, x, core).
Axes of the slice: x: 2, y: 2, z: 4, core: 2. Of those that a mesh axis runs over, the one named last changes fastest.
Arguments:
- tokens: bfloat16 [32768, 768], P(('dp', 'shard')), may hold values from -6 to 6
- cotangent: bfloat16 [32768, 768], P(('dp', 'shard')), may hold values from -6 to 6
- lengths: int32 [32], P(('dp', 'shard')), may hold values from 341 to 1024, as said below
- attn_gain: bfloat16 [768], P(('dp', 'shard')), may hold values from 0.5 to 1.5
- attn_shift: bfloat16 [768], P(('dp', 'shard')), may hold values from -1.5 to 1.5
- qkv_weight: bfloat16 [768, 2304], P(('dp', 'shard')), may hold values from -0.21875 to 0.21875
- qv_bias: bfloat16 [2, 768], P(None, ('dp', 'shard')), may hold values from -1.5 to 1.5
- proj_weight: bfloat16 [768, 768], P(('dp', 'shard')), may hold values from -3.5 to 3.5
- proj_bias: bfloat16 [768], P(('dp', 'shard')), may hold values from -1.5 to 1.5
- mlp_gain: bfloat16 [768], P(('dp', 'shard')), may hold values from 0.5 to 1.5
- mlp_shift: bfloat16 [768], P(('dp', 'shard')), may hold values from -1.5 to 1.5
- up_weight: bfloat16 [768, 3072], P(('dp', 'shard')), may hold values from -0.21875 to 0.21875
- up_bias: bfloat16 [3072], P(('dp', 'shard')), may hold values from -1.5 to 1.5
- down_weight: bfloat16 [3072, 768], P(('dp', 'shard')), may hold values from -0.109375 to 0.109375
- down_bias: bfloat16 [768], P(('dp', 'shard')), may hold values from -1.5 to 1.5
Outputs:
- block_out: bfloat16 [32768, 768], P(('dp', 'shard'))
- input_grad: bfloat16 [32768, 768], P(('dp', 'shard'))
- grad_attn_gain: float32 [768], P(('dp', 'shard'))
- grad_attn_shift: float32 [768], P(('dp', 'shard'))
- grad_qkv_weight: float32 [768, 2304], P(('dp', 'shard'))
- grad_qv_bias: float32 [2, 768], P(None, ('dp', 'shard'))
- grad_proj_weight: float32 [768, 768], P(('dp', 'shard'))
- grad_proj_bias: float32 [768], P(('dp', 'shard'))
- grad_mlp_gain: float32 [768], P(('dp', 'shard'))
- grad_mlp_shift: float32 [768], P(('dp', 'shard'))
- grad_up_weight: float32 [768, 3072], P(('dp', 'shard'))
- grad_up_bias: float32 [3072], P(('dp', 'shard'))
- grad_down_weight: float32 [3072, 768], P(('dp', 'shard'))
- grad_down_bias: float32 [768], P(('dp', 'shard'))
Inputs may be any that keep to these rules, and one draw needn't show every extreme that they name: `lengths`: A clip holds 1024 valid patches (full clip) or 341 to 1024 // 2 (patchout clip); slots from the count on are padding whose keys are masked.
All inputs are finite; a program needn't handle non-finite values.
Results may differ from a plain program's by a relative error of at most 0.012.
Values may be sent and summed in bfloat16 or wider, within the bound.
A program may use at most 256 MiB of HBM per device.

v0:
```python
import functools

import jax
import jax.numpy as jnp
from jax import lax
from jax.experimental import pallas as pl
from jax.experimental.pallas import tpu as pltpu
from jax.sharding import PartitionSpec as P

f32 = jnp.float32
bf16 = jnp.bfloat16
HD = 64
PAIR = 2 * HD
EPS = 1e-06
MASKED = -1e30
AXES = ("dp", "shard")
VMEM_LIMIT = 65280 * 2**10

AG, AS, QB, VB, PB, MG, MS, DB, UB = range(9)


def dg(a, b, ca, cb):
    return lax.dot_general(a, b, (((ca,), (cb,)), ((), ())), preferred_element_type=f32)


def rows_of(v):
    return v.reshape(-1, v.shape[-1])


def norm_parts(v):
    center = v - jnp.mean(v, -1, keepdims=True)
    inv = lax.rsqrt(jnp.mean(center * center, -1, keepdims=True) + EPS)
    return center * inv, inv


def norm_back(n, inv, z):
    return inv * (z - jnp.mean(z, -1, keepdims=True) - n * jnp.mean(z * n, -1, keepdims=True))


def key_bias(length, seq):
    return jnp.where(lax.broadcasted_iota(jnp.int32, (seq, 1), 0) < length, 0.0, MASKED).astype(f32)


def head_only(v, hh):
    lane = lax.broadcasted_iota(jnp.int32, (1, PAIR), 1)
    return jnp.where(lane // HD == hh, v, jnp.zeros((), v.dtype))


class Place:
    def __init__(self, nz):
        shard = lax.axis_index("shard")
        self.nz = nz
        self.y = lax.axis_index("dp")
        self.c = lax.rem(shard, 2)
        self.x = lax.rem(lax.div(shard, 2), 2)
        self.z = lax.div(shard, 4)
        fy, fx = 1 - 2 * self.y, 1 - 2 * self.x
        self.ay, self.ax = self.y + (1 - self.c) * fy, self.x + self.c * fx
        self.by, self.bx = self.y + self.c * fy, self.x + (1 - self.c) * fx

    def device(self, y, z, x, c):
        return (y, (z * 2 + x) * 2 + c)

    def peer(self):
        return self.device(self.y, self.z, self.x, 1 - self.c)

    def along_z(self, k):
        return self.device(self.y, lax.rem(self.z + k, self.nz), self.x, self.c)

    def a(self):
        return self.device(self.ay, self.z, self.ax, self.c)

    def b(self):
        return self.device(self.by, self.z, self.bx, self.c)

    def partners(self):
        return [self.peer(), self.a(), self.b()] + [self.along_z(k) for k in range(1, self.nz)]


def enter(place):
    barrier = pltpu.get_barrier_semaphore()
    partners = place.partners()
    for d in partners:
        pl.semaphore_signal(barrier, inc=1, device_id=d, device_id_type=pl.DeviceIdType.MESH)
    pl.semaphore_wait(barrier, len(partners))


def remote(src, dst, send, recv, device):
    return pltpu.make_async_remote_copy(
        src_ref=src, dst_ref=dst, send_sem=send, recv_sem=recv, device_id=device,
        device_id_type=pl.DeviceIdType.MESH,
    )


class Gather:
    def __init__(self, place, block, column, swap, send, recv):
        self.p, self.block, self.column, self.swap = place, block, column, swap
        self.send, self.recv = send, recv
        self.started = []

    def move(self, slot, src, dst, device):
        return remote(src, dst, self.send.at[slot], self.recv.at[slot], device)

    def go(self, copy):
        copy.start()
        self.started.append(copy)

    def exchange(self):
        src, dst, _ = self.swap
        return self.move(0, src, dst, self.p.peer())

    def X(self):
        self.go(self.exchange())

    def zs(self):
        p = self.p
        own = self.block(p.y, p.z, p.x, p.c)
        return [self.move(k, own, own, p.along_z(k)) for k in range(1, p.nz)]

    def over(self, slot, y, x, device):
        v = self.column(y, x, self.p.c)
        return self.move(slot, v, v, device)

    def to_b(self):
        return self.over(4, self.p.y, self.p.x, self.p.b())

    def to_a(self, second):
        p = self.p
        y, x = (p.by, p.bx) if second else (p.y, p.x)
        return self.over(5 + second, y, x, p.a())

    def across(self, i):
        p = self.p
        y, x = [(p.y, p.x), (p.by, p.bx), (p.ay, p.ax), (1 - p.y, 1 - p.x)][i]
        return self.over(7 + i, y, x, p.peer())

    def Z(self):
        if self.swap is not None:
            self.exchange().wait()
            self.swap[2]()
        for cp in self.zs():
            self.go(cp)

    def B(self):
        for cp in self.zs():
            cp.wait_recv()
        self.go(self.to_b())
        self.go(self.to_a(0))
        self.go(self.across(0))

    def A(self):
        self.to_b().wait_recv()
        self.go(self.to_a(1))
        self.go(self.across(1))

    def C(self):
        self.to_a(0).wait_recv()
        self.go(self.across(2))
        self.to_a(1).wait_recv()
        self.go(self.across(3))

    def D(self):
        for i in range(4):
            self.across(i).wait_recv()

    def finish(self):
        for cp in self.zs() + [self.to_b(), self.to_a(0), self.to_a(1)] + [self.across(i) for i in range(4)]:
            cp.wait_send()


class Scatter:
    def __init__(self, place, own, other, bufs, send, recv, total):
        self.p, self.own, self.other = place, own, other
        self.r0, self.r1, self.r2, self.r3 = bufs
        self.send, self.recv, self.total = send, recv, total

    def move(self, slot, src, dst, device):
        return remote(src, dst, self.send.at[slot], self.recv.at[slot], device)

    def swap(self):
        return self.move(0, self.other, self.r0, self.p.peer())

    def to_a(self, i):
        p = self.p
        src = self.own.at[p.ay, :, p.ax] if i == 0 else self.own.at[1 - p.y, :, 1 - p.x]
        return self.move(1 + i, src, self.r1.at[i], p.a())

    def to_b(self):
        p = self.p
        return self.move(3, self.own.at[p.by, :, p.bx], self.r2, p.b())

    def to_z(self, k):
        p = self.p
        return self.move(3 + k, self.own.at[p.y, lax.rem(p.z + k, p.nz), p.x], self.r3.at[k - 1], p.along_z(k))

    def add(self, y, x, other):
        self.own[y, :, x] = self.own[y, :, x] + other

    def S0(self):
        self.swap().start()

    def S1(self):
        p = self.p
        self.swap().wait()
        for i, (y, x) in enumerate([(p.ay, p.ax), (1 - p.y, 1 - p.x), (p.by, p.bx), (p.y, p.x)]):
            self.add(y, x, self.r0[y, :, x])
            if i < 2:
                self.to_a(i).start()

    def S2(self):
        p = self.p
        self.to_a(1).wait_recv()
        self.add(p.by, p.bx, self.r1[1])
        self.to_b().start()
        self.to_a(0).wait_recv()
        self.add(p.y, p.x, self.r1[0])

    def S3(self):
        p = self.p
        self.to_b().wait_recv()
        self.add(p.y, p.x, self.r2[...])
        for k in range(1, p.nz):
            self.to_z(k).start()

    def S4(self):
        p = self.p
        total = self.own[p.y, p.z, p.x].astype(f32)
        for k in range(1, p.nz):
            self.to_z(k).wait_recv()
            total += self.r3[k - 1].astype(f32)
        self.total(total)

    def finish(self):
        for cp in [self.to_a(0), self.to_a(1), self.to_b()] + [
            self.to_z(k) for k in range(1, self.p.nz)
        ]:
            cp.wait_send()


class Handover:
    def __init__(self, place, stage, landing, write, send, recv):
        self.p, self.stage, self.landing, self.write = place, stage, landing, write
        self.copy = remote(stage, landing, send, recv, place.peer())

    def start(self, total):
        own = total.shape[0] // 2
        top, bottom = total[:own], total[own:]
        self.stage[...] = jnp.where(self.p.c == 0, bottom, top)
        self.copy.start()
        self.write(self.p.c, jnp.where(self.p.c == 0, top, bottom))

    def S5(self):
        self.copy.wait_recv()
        self.write(1 - self.p.c, self.landing[...])

    def end(self):
        self.copy.wait_send()


class VectorSum:
    def __init__(self, place, value, bufs, send, recv):
        self.p, self.value, self.bufs, self.send, self.recv = place, value, bufs, send, recv

    def move(self, slot):
        p = self.p
        device = [p.peer(), p.a(), p.b()][slot] if slot < 3 else p.along_z(slot - 2)
        return remote(
            self.value.at[min(slot, 3)], self.bufs.at[slot], self.send.at[slot], self.recv.at[slot], device
        )

    def S0(self):
        self.move(0).start()

    def step(self, slot):
        self.move(slot - 1).wait_recv()
        self.value[slot] = self.value[slot - 1] + self.bufs[slot - 1]
        for k in range(self.p.nz - 1 if slot == 3 else 1):
            self.move(slot + k).start()

    def S1(self):
        self.step(1)

    def S2(self):
        self.step(2)

    def S3(self):
        self.step(3)

    def S4(self):
        total = self.value[3]
        for k in range(self.p.nz - 1):
            self.move(3 + k).wait_recv()
            total += self.bufs[3 + k]
        self.value[4] = total

    def finish(self):
        for slot in range(2 + self.p.nz):
            self.move(slot).wait_send()


def expand_table(vbuf, vec, ub, own, piece):
    many = vbuf.shape[0] * vbuf.shape[1] * vbuf.shape[2] * vbuf.shape[3]
    flat = vbuf[...].reshape(many * 16, PAIR)

    def spread(n, each, first=0):
        lane = lax.broadcasted_iota(jnp.int32, (PAIR, n), 1)
        row = lax.broadcasted_iota(jnp.int32, (PAIR, n), 0) - first
        return (lax.rem(lane, each) == row).astype(f32).astype(bf16)

    def mine(full, each):
        shape = (many,) + (1,) * (full.ndim - 2) + full.shape[-1:]
        where = lax.broadcasted_iota(jnp.int32, shape, len(shape) - 1) - each * lax.broadcasted_iota(
            jnp.int32, shape, 0
        )
        return jnp.where((where >= 0) & (where < each), full, 0.0)

    full = dg(flat, spread(vec.shape[1], own), 1, 0).reshape(many, 16, vec.shape[1])
    vec[...] = jnp.sum(mine(full, own), 0)
    pick = (
        lax.broadcasted_iota(jnp.int32, (many, many * 16), 1)
        == 16 * lax.broadcasted_iota(jnp.int32, (many, many * 16), 0) + 8
    )
    row = dg(pick.astype(f32).astype(bf16), flat, 1, 0).astype(bf16)
    for i in range(ub.shape[0]):
        full = dg(row, spread(ub.shape[2], piece, i * piece), 1, 0)
        ub[i] = jnp.sum(mine(full, piece), 0, keepdims=True)


def regroup(pieces, piece):
    n = pieces * PAIR
    src = lax.broadcasted_iota(jnp.int32, (n, n), 0)
    dst = lax.broadcasted_iota(jnp.int32, (n, n), 1)
    inner = lax.rem(dst, PAIR)
    want = lax.div(inner, piece) * (pieces * piece) + lax.div(dst, PAIR) * piece + lax.rem(inner, piece)
    return (src == want).astype(f32)


def gather_items(place, own_down, wqkv, wproj, wup, wdown, vbuf, xs, xr, send, recv):
    p = place
    (xs_qkv, xs_proj, xs_up), (xr_qkv, xr_proj, xr_up) = xs, xr
    own = wqkv.shape[-2] // 2

    def joined(mine, theirs, write):
        def go():
            m, t = mine()[:own].astype(f32), theirs()[:own].astype(f32)
            lo, hi = jnp.where(p.c == 0, m, t), jnp.where(p.c == 0, t, m)
            write(jnp.concatenate([lo, hi], 0).astype(bf16))
        return go

    items = []

    def add(block, column, swap):
        i = len(items)
        items.append(Gather(p, block, column, swap, send.at[i], recv.at[i]))

    add(lambda y, z, x, c: vbuf.at[y, z, x, c], lambda y, x, c: vbuf.at[y, :, x, c], None)

    def add_swapped(view, xs_of, xr_of):
        block = lambda y, z, x, c: view(c).at[y, z, x]
        column = lambda y, x, c: view(c).at[y, :, x]

        def write(v):
            view(p.c)[p.y, p.z, p.x] = v

        add(block, column, (xs_of(1 - p.c), xr_of, joined(lambda: xs_of(p.c)[...], lambda: xr_of[...], write)))

    for g in range(wqkv.shape[0]):
        add_swapped(lambda c, g=g: wqkv.at[g, c], lambda c, g=g: xs_qkv(g, c), xr_qkv.at[g])
    add_swapped(lambda c: wproj.at[c], xs_proj, xr_proj)
    for k in range(wup.shape[0]):
        add(
            lambda y, z, x, c, k=k: wdown.at[k, y, z, x, c],
            lambda y, x, c, k=k: wdown.at[k, y, :, x, c],
            None,
        )
        add_swapped(lambda c, k=k: wup.at[k, c], lambda c, k=k: xs_up(k, c), xr_up.at[k])
    return items


def slice_lanes(v, first, count):
    lane = lax.broadcasted_iota(jnp.int32, (v.shape[1], PAIR), 0) - first
    out = lax.broadcasted_iota(jnp.int32, (v.shape[1], PAIR), 1)
    pick = ((lane == out) & (out < count)).astype(f32)
    return lax.dot_general(
        v, pick, (((1,), (0,)), ((), ())), precision=lax.Precision.HIGHEST, preferred_element_type=f32
    )


def attend(k2, v2t, q2, bias_k, write):
    ones = jnp.ones((16, k2.shape[0]), bf16)
    for hh in range(2):
        s = dg(k2, head_only(q2, hh), 1, 1) + bias_k
        top = jnp.max(s, 0, keepdims=True)
        e = jnp.exp(s - top).astype(bf16)
        o = dg(jnp.concatenate([v2t[HD * hh : HD * hh + HD], ones], 0), e, 1, 0)
        total = o[HD : HD + 1]
        write(hh, o[:HD] / total, top + jnp.log(total))


def attend_back(q_of, k2, v2, do_of, ot_of, lse_of, bias_k, block, between):
    seq = k2.shape[0]
    scale = HD**-0.5
    k2t = k2.T
    dk = dv = None
    dqt = []
    for hh in range(2):
        rows = slice(HD * hh, HD * hh + HD)
        parts = []
        for i in range(seq // block):
            sl = slice(i * block, (i + 1) * block)
            qm = head_only(q_of(sl) * jnp.asarray(scale, bf16), hh)
            d = do_of(sl)
            dm = head_only(d, hh)
            delta = jnp.sum(d.astype(f32).T[rows] * ot_of(rows, sl).astype(f32), 0, keepdims=True)
            e = jnp.exp(dg(k2, qm, 1, 1) + bias_k - lse_of(hh, sl))
            ds = (e * (dg(v2, dm, 1, 1) - delta)).astype(bf16)
            t = dg(e.astype(bf16), dm, 1, 0)
            dv = t if dv is None else dv + t
            t = dg(ds, qm, 1, 0)
            dk = t if dk is None else dk + t
            parts.append(dg(k2t[rows], ds, 1, 0) * scale)
        dqt.append(jnp.concatenate(parts, 1))
        if hh == 0:
            between()
    return jnp.concatenate(dqt, 0), dk, dv


def up_step(n2, cot, up, down, up_bias):
    h = dg(n2, up(), 1, 0) + up_bias
    phi = 0.5 * (1.0 + lax.erf(h * 0.7071067811865476))
    a = (h * phi).astype(bf16)
    ga = dg(cot, down(), 1, 1)
    g = (ga * (phi + h * jnp.exp(-0.5 * h * h) * 0.3989422804014327)).astype(bf16)
    return a, g


def pick(index, choices):
    v = choices[0]
    for i in range(1, len(choices)):
        v = jnp.where(index == i, choices[i], v)
    return v


def blocks(count, size, body):
    @pl.loop(0, count)
    def _(r):
        body(r, pl.ds(pl.multiple_of(r * size, size), size))


VECI, G0, G1, G2, PROJ, D0, U0, D1, U1, D2, U2 = range(11)
SV1, SD0, SU0, SD1, SU1, SD2, SU2, SP, SG0, SG1, SG2, SV2 = range(20, 32)
PLAN = {
    "stats": [("B", VECI), ("B", G0), ("Z", G2), ("A", VECI), ("B", G1), ("A", G0), ("C", VECI), ("D", VECI)],
    "norm": [("Z", PROJ), ("C", G0), ("B", G2), ("A", G1), ("Z", D0), ("D", G0)],
    "f0": [("Z", U0), ("C", G1), ("A", G2), ("B", PROJ), ("B", D0)],
    "f1": [("Z", D1), ("D", G1), ("C", G2), ("A", PROJ), ("B", U0)],
    "f2": [("Z", U1), ("C", PROJ), ("A", D0), ("B", D1)],
    "f3": [("Z", D2), ("D", G2), ("A", U0), ("B", U1), ("C", D0)],
    "f4": [("Z", U2), ("A", D1), ("C", U0)],
    "f5": [("B", D2), ("D", PROJ), ("D", D0), ("C", D1)],
    "m0": [("D", U0), ("A", U1), ("B", U2)],
    "m0g": [("finish", D0), ("finish", U0)],
    "m1": [("A", D2), ("C", U1), ("D", D1)],
    "m2": [("S0", SD0), ("S0", SU0), ("D", U1), ("A", U2), ("C", D2)],
    "m2g": [("finish", D1), ("finish", U1)],
    "m3": [("C", U2), ("D", D2), ("S1", SD0), ("S1", SU0)],
    "m4": [("S0", SD1), ("S0", SU1), ("D", U2), ("S2", SD0)],
    "m4g": [("finish", D2), ("finish", U2)],
    "m5": [("S1", SD1), ("S2", SU0)],
    "m6": [("S0", SD2), ("S0", SU2), ("S1", SU1), ("S3", SD0), ("S2", SD1), ("finish", PROJ)],
    "mid": [("S0", SP), ("S0", SV1), ("S1", SD2), ("S3", SU0), ("S4", SD0), ("S2", SU1)],
    "b0h": [("S1", SU2), ("S3", SD1), ("S1", SV1)],
    "b0": [("S1", SP), ("S2", SD2), ("S3", SU1), ("S4", SU0), ("S2", SV1)],
    "b1h": [("S4", SD1), ("S5", SU0), ("S3", SV1)],
    "b1": [("S0", SG0), ("S2", SU2), ("S4", SU1), ("S4", SV1)],
    "b2h": [("S1", SG0), ("S2", SP), ("S3", SD2), ("S5", SU1), ("S3", SU2)],
    "b2": [("S4", SD2)],
    "b3h": [("S2", SG0), ("S3", SP), ("S4", SU2)],
    "b3": [("S0", SG1), ("S3", SG0), ("S5", SU2), ("S4", SP)],
    "b4h": [("S1", SG1), ("S5", SP)],
    "b4": [("S4", SG0)],
    "b5h": [("S2", SG1), ("S5", SG0)],
    "b5": [("S0", SG2), ("S3", SG1)],
    "r0": [("S1", SG2)],
    "r1": [("S4", SG1)],
    "r2": [("S5", SG1)],
    "r3": [("S0", SV2), ("S2", SG2)],
    "end": [("S1", SV2), ("S3", SG2), ("S2", SV2), ("S3", SV2), ("S4", SG2), ("S4", SV2), ("S5", SG2)],
}


def layer_kernel(
    len_ref, tok_hbm, cot_ref, vec_in, wqkv_in, wproj_in, wup_in, wdown_in,
    out_hbm, gin_hbm, oqkv, oproj, oup, odown, vg_out,
    n1, n1t, proj, ot, att, lse, res, n2t, acc, gn2, gh,
    vec_ref, ub_ref, wqkv, wproj, wup, wdown, vbuf, xr_qkv, xr_proj, xr_up, gsend, grecv,
    vsum, up0, up1, up2, up3, down0, down1, down2, down3, proj0, proj1, proj2, proj3, qkv1, qkv2, qkv3,
    qkv0, stage_up, stage_proj, stage_qkv, land_up, land_proj, land_qkv, vbufs, send, recv, hsend, hrecv, sems,
):
    seq, width = cot_ref.shape
    half = width // 2
    pairs = proj.shape[0]
    own, rows = wqkv_in.shape[0], wdown_in.shape[0]
    groups, pieces = wqkv.shape[0], wup.shape[0]
    piece = rows // pieces
    sub = wup.shape[-1]
    place = Place(wqkv.shape[3])
    p_ = place
    n2, act, gin, tok_early, tok_late = n1, att, att, gh, n1
    vg_one, vg_two = vsum.at[0, 0], vsum.at[1, 0]

    def own_gradient(g):
        return up0.at[g, :, :, :, :, pl.ds(0, 3 * PAIR)]

    def other_gradient(g):
        return wup.at[g, 1 - place.c, :, :, :, :, pl.ds(0, 3 * PAIR)]


    padded = xr_proj.shape[0]

    def staged(first, lanes):
        return lambda i, c: n2t.at[pl.ds(pl.multiple_of((first + 2 * i + c) * padded, padded), padded), 0:lanes]

    xs_qkv, xs_up = staged(0, 3 * PAIR), staged(2 * groups, sub)
    xs_proj = functools.partial(staged(2 * (groups + pieces), half), 0)

    items = dict(enumerate(gather_items(
        place, wdown_in, wqkv, wproj, wup, wdown, vbuf, (xs_qkv, xs_proj, xs_up), (xr_qkv, xr_proj, xr_up),
        gsend, grecv,
    )))
    handovers = []

    def add(i, own_half, other_half, bufs, total):
        k = i - SV1
        items[i] = Scatter(p_, own_half, other_half, bufs, send.at[k], recv.at[k], total)

    def add_shared(i, own_half, other_half, bufs, stage, landing, write):
        k = i - SV1
        h = Handover(p_, stage, landing, write, hsend.at[k], hrecv.at[k])
        handovers.append(h)
        add(i, own_half, other_half, bufs, h.start)
        items[i].S5 = h.S5

    for k in range(pieces):

        def write_down(total, k=k):
            odown[k * piece : (k + 1) * piece, :] = total

        add(
            SD0 + 2 * k, wdown.at[k, :, :, :, p_.c], wdown.at[k, :, :, :, 1 - p_.c],
            (down0.at[k], down1.at[k], down2.at[k], down3.at[k]), write_down,
        )

        def write_up(c, v, k=k):
            back = regroup(pieces, piece)[:, k * PAIR : (k + 1) * PAIR]
            for i in range(sub // PAIR):
                lanes = pl.ds(pl.multiple_of((c * (sub // PAIR) + i) * pieces * PAIR, PAIR), pieces * PAIR)
                oup[:, lanes] += lax.dot_general(
                    v[:, i * PAIR : (i + 1) * PAIR], back, (((1,), (1,)), ((), ())),
                    precision=lax.Precision.HIGHEST, preferred_element_type=f32,
                )

        add_shared(
            SU0 + 2 * k, wup.at[k, p_.c], wup.at[k, 1 - p_.c], (up0.at[k], up1.at[k], up2.at[k], up3.at[k]),
            stage_up.at[k], land_up.at[k], write_up,
        )

    def write_proj(c, v):
        oproj[:, pl.ds(pl.multiple_of(c * half, PAIR), half)] = v

    add_shared(SP, wproj.at[p_.c], wproj.at[1 - p_.c], (proj0, proj1, proj2, proj3), stage_proj, land_proj, write_proj)
    for g in range(groups):

        def write_qkv(c, v, g=g):
            for t in range(3):
                oqkv[:, pl.ds(pl.multiple_of(t * width + (2 * g + c) * PAIR, PAIR), PAIR)] = v[
                    :, t * PAIR : (t + 1) * PAIR
                ]

        add_shared(
            SG0 + g, own_gradient(g), other_gradient(g),
            (qkv0.at[g], qkv1.at[g], qkv2.at[g], qkv3.at[g]), stage_qkv.at[g], land_qkv.at[g], write_qkv,
        )
    for i, v in ((SV1, 0), (SV2, 1)):
        items[i] = VectorSum(p_, vsum.at[v], vbufs.at[v], send.at[i - SV1], recv.at[i - SV1])
    finished = set()

    def tick(name):
        for step, i in PLAN.get(name, ()):
            getattr(items[i], step)()
            if step == "finish":
                finished.add(i)

    def ticks(index, names):
        for i, name in enumerate(names):
            if PLAN.get(name):

                @pl.when(index == i)
                def _(name=name):
                    tick(name)

    def w_qkv(p):
        return rows_of(wqkv[lax.div(p, 2), lax.rem(p, 2)])

    def w_up(k, u):
        return rows_of(wup[k, u])

    def w_down(k, u):
        return rows_of(wdown[k, u])

    def w_proj(i):
        return rows_of(wproj[i])

    def vec(i):
        return vec_ref[i : i + 1, :]

    rb = 256
    nb = seq // rb
    tok_copy = pltpu.make_async_copy(tok_hbm, tok_early, sems.at[1])
    tok_copy.start()
    vbuf[p_.y, p_.z, p_.x, p_.c] = vec_in[...]
    for p in range(pairs):
        for t in range(3):
            lanes = slice(t * width + p * PAIR, t * width + (p + 1) * PAIR)
            n2t[p * padded : p * padded + own, t * PAIR : (t + 1) * PAIR] = wqkv_in[:, lanes]
    enter(place)
    for i in (G0, G1, G2):
        items[i].X()
    items[VECI].Z()
    items[G0].Z()
    for i in range(2):
        row = (2 * (groups + pieces) + i) * padded
        n2t[row : row + own, 0:half] = wproj_in[:, i * half : (i + 1) * half]
    order = regroup(pieces, piece).astype(bf16)
    for i in range(2 * sub // PAIR):
        u, q = divmod(i, sub // PAIR)
        v = dg(wup_in[:, i * pieces * PAIR : (i + 1) * pieces * PAIR], order, 1, 0).astype(bf16)
        for k in range(pieces):
            row = (2 * (groups + k) + u) * padded
            n2t[row : row + own, q * PAIR : (q + 1) * PAIR] = v[:, k * PAIR : (k + 1) * PAIR]
    items[G1].Z()
    for i in (PROJ, U0, U1, U2):
        items[i].X()
    for k in range(pieces):
        wdown[k, p_.y, p_.z, p_.x, p_.c] = wdown_in[k * piece : (k + 1) * piece, :]
    oup[...] = jnp.zeros(oup.shape, f32)
    tok_copy.wait()

    def stats(r, sl):
        res[sl, :] = norm_parts(tok_early[sl, :].astype(f32))[0]

    blocks(nb, rb, stats)
    tick("stats")
    expand_table(vbuf, vec_ref, ub_ref, own, piece)

    def norm(r, sl):
        n1[sl, :] = (res[sl, :] * vec(AG) + vec(AS)).astype(bf16)

    blocks(nb, rb, norm)
    n1t[...] = n1[...].T
    tick("norm")

    bias_k = key_bias(len_ref[0], seq)
    q_bias = [vec(QB)[:, i * PAIR : (i + 1) * PAIR] for i in range(pairs)]
    v_bias = [vec(VB)[:, i * PAIR : (i + 1) * PAIR] for i in range(pairs)]

    @pl.loop(0, pairs)
    def _(p):
        qkv = dg(n1[...], w_qkv(p), 1, 0)
        proj[p, :, 0:PAIR] = (qkv[:, 0:PAIR] + pick(p, q_bias)).astype(bf16)
        proj[p, :, PAIR : 2 * PAIR] = qkv[:, PAIR : 2 * PAIR].astype(bf16)
        proj[p, :, 2 * PAIR :] = (qkv[:, 2 * PAIR :] + pick(p, v_bias)).astype(bf16)

        def write(hh, o, total):
            ot[p, HD * hh : HD * hh + HD, :] = o.astype(bf16)
            lse[pl.ds(2 * p + hh, 1), :] = total

        attend(
            proj[p, :, PAIR : 2 * PAIR], proj[p, :, 2 * PAIR :].T,
            proj[p, :, 0:PAIR] * jnp.asarray(HD**-0.5, bf16), bias_k, write,
        )
        ticks(p, [f"f{i}" for i in range(pairs)])

    for p in range(pairs):
        att[:, p * PAIR : (p + 1) * PAIR] = ot[p].T

    def branch(r, sl):
        a = att[sl, :]
        v = tok_early[sl, :].astype(f32) + vec(PB)
        v += jnp.concatenate([dg(a, w_proj(i), 1, 0) for i in range(2)], 1)
        res[sl, :] = v
        acc[sl, :] = v + vec(DB)
        gn2[sl, :] = jnp.zeros((rb, width), f32)
        n2[sl, :] = (norm_parts(v)[0] * vec(MG) + vec(MS)).astype(bf16)

    blocks(nb, rb, branch)
    n2t[...] = n2[...].T

    rm = 512
    @pl.loop(0, 2 * pieces)
    def _(turn):
        k, u = lax.div(turn, 2), lax.rem(turn, 2)
        cols = pl.ds(pl.multiple_of(u * sub, PAIR), sub)
        total = pl.ds(4 + k, 1)
        ticks(turn, [f"m{i}" for i in range(2 * pieces)])
        vg_one[total, cols] = jnp.zeros((1, sub), f32)

        def stage_one(r, sl):
            a, g = up_step(n2[sl, :], cot_ref[sl, :], lambda: w_up(k, u), lambda: w_down(k, u), ub_ref[k, :, cols])
            act[sl, 0:sub] = a
            gh[sl, 0:sub] = g
            acc[sl, :] += dg(a, w_down(k, u), 1, 0)
            gn2[sl, :] += dg(g, w_up(k, u), 1, 1)
            vg_one[total, cols] += jnp.sum(g.astype(f32), 0, keepdims=True)

        blocks(seq // rm, rm, stage_one)
        ticks(turn, [f"m{i}g" for i in range(2 * pieces)])
        v = dg(act[:, 0:sub], cot_ref[...], 0, 0).astype(bf16)
        wdown[k, u] = v.reshape(wdown.shape[2:])
        wup[k, u] = dg(n2t[...], gh[:, 0:sub], 1, 0).astype(bf16).reshape(wup.shape[2:])

    tick(f"m{2 * pieces}")

    vg_one[0:4, :] = jnp.zeros((4, vg_one.shape[1]), f32)
    vg_one[7:8, :] = jnp.zeros((1, vg_one.shape[1]), f32)

    def back_two(r, sl):
        n2[sl, :] = acc[sl, :].astype(bf16)
        g = gn2[sl, :]
        n, inv = norm_parts(res[sl, :])
        cot = cot_ref[sl, :].astype(f32)
        mid = cot + norm_back(n, inv, g * vec(MG))
        acc[sl, :] = mid
        low = mid.astype(bf16)
        act[sl, :] = low
        vg_one[0:1, 0:width] += jnp.sum(g * n, 0, keepdims=True)
        vg_one[1:2, 0:width] += jnp.sum(g, 0, keepdims=True)
        vg_one[2:3, 0:width] += jnp.sum(low.astype(f32), 0, keepdims=True)
        vg_one[3:4, 0:width] += jnp.sum(cot, 0, keepdims=True)
        back = dg(low[:, :half], w_proj(0), 1, 1) + dg(low[:, half:], w_proj(1), 1, 1)
        gh[sl, :] = back.astype(bf16)

    blocks(nb, rb, back_two)
    out_copy = pltpu.make_async_copy(n2, out_hbm, sems.at[0])
    out_copy.start()
    for i in range(2):
        v = dg(rows_of(ot[...]), act[:, i * half : (i + 1) * half], 1, 0).astype(bf16)
        wproj[i] = v.reshape(wproj.shape[1:])
    vg_two[...] = jnp.zeros(vg_two.shape, f32)
    tick("mid")

    def weight_gradient(p, dst):
        g = proj[p]
        cols = pl.ds(pl.multiple_of(p * PAIR, PAIR), PAIR)
        sums = jnp.sum(g.astype(f32), 0, keepdims=True)
        vg_two[2:3, cols] = sums[:, 0:PAIR]
        vg_two[3:4, cols] = sums[:, 2 * PAIR :]
        dst[...] = dg(n1t[...], g, 1, 0).astype(bf16).reshape(dst.shape)

    @pl.loop(0, pairs)
    def _(p):
        lanes = pl.ds(pl.multiple_of(p * PAIR, PAIR), PAIR)
        dqt, dk, dv = attend_back(
            lambda sl: proj[p, sl, 0:PAIR],
            proj[p, :, PAIR : 2 * PAIR],
            proj[p, :, 2 * PAIR :],
            lambda sl: gh[sl, lanes],
            lambda rows, sl: ot[p, rows, sl],
            lambda hh, sl: lse[pl.ds(2 * p + hh, 1), sl],
            bias_k,
            512,
            lambda: ticks(p, [f"b{i}h" for i in range(pairs)]),
        )
        proj[p, :, 0:PAIR] = dqt.T.astype(bf16)
        proj[p, :, PAIR : 2 * PAIR] = dk.astype(bf16)
        proj[p, :, 2 * PAIR :] = dv.astype(bf16)

        @pl.when(lax.rem(p, 2) == 1)
        def _():
            g = lax.div(p, 2)
            weight_gradient(2 * g + p_.c, own_gradient(g))
            weight_gradient(2 * g + 1 - p_.c, other_gradient(g))

        ticks(p, [f"b{i}" for i in range(pairs)])

    out_copy.wait()
    tok_copy = pltpu.make_async_copy(tok_hbm, tok_late, sems.at[0])
    tok_copy.start()
    tok_copy.wait()

    def back_one(r, sl):
        g = dg(proj[0, sl, :], rows_of(wqkv[0, 0]), 1, 1)
        for p in range(1, pairs):
            g += dg(proj[p, sl, :], rows_of(wqkv[p // 2, p % 2]), 1, 1)
        n, inv = norm_parts(tok_late[sl, :].astype(f32))
        gin[sl, :] = (acc[sl, :] + norm_back(n, inv, g * vec(AG))).astype(bf16)
        vg_two[0:1, 0:width] += jnp.sum(g * n, 0, keepdims=True)
        vg_two[1:2, 0:width] += jnp.sum(g, 0, keepdims=True)
        ticks(r, [f"r{i}" for i in range(nb)])

    blocks(nb, rb, back_one)
    gin_copy = pltpu.make_async_copy(gin, gin_hbm, sems.at[1])
    gin_copy.start()
    index = ((p_.y * p_.nz + p_.z) * 2 + p_.x) * 2 + p_.c
    one = vsum[0, 4]
    vg_out[0:8, :] = slice_lanes(one, index * own, own)
    vg_out[4:7, :] = slice_lanes(one, index * piece, piece)[4:7]
    tick("end")
    vg_out[8:16, :] = slice_lanes(vsum[1, 4], index * own, own)
    for i, item in items.items():
        if i not in finished:
            item.finish()
    for h in handovers:
        h.end()
    gin_copy.wait()


def forward_kernel(
    len_ref, tok_ref, cot_ref, vec_ref, wqkv, wproj, wup, wdown,
    out_hbm, proj_hbm, ot_hbm, lse_hbm, do_hbm, gmid_hbm, n1t_hbm, gup_hbm, gdown_hbm, gproj_hbm, vg_ref,
    n1, n1t, proj, ot, att, lse, res, n2, n2t, acc, gn2, act, gh, gstage, sems,
):
    seq, width = tok_ref.shape
    half = width // 2
    chunks, pairs = gup_hbm.shape[0], proj.shape[0]
    copies = []

    def send_out(src, dst, sem):
        cp = pltpu.make_async_copy(src, dst, sem)
        cp.start()
        copies.append(cp)

    def vec(i):
        return vec_ref[i : i + 1, :]

    rb = 256
    nb = seq // rb

    def norm(r, sl):
        n1[sl, :] = (norm_parts(tok_ref[sl, :].astype(f32))[0] * vec(AG) + vec(AS)).astype(bf16)

    blocks(nb, rb, norm)
    n1t[...] = n1[...].T
    send_out(n1t, n1t_hbm, sems.at[0])
    bias_k = key_bias(len_ref[0], seq)
    q_bias = [vec(QB)[:, i * PAIR : (i + 1) * PAIR] for i in range(pairs)]
    v_bias = [vec(VB)[:, i * PAIR : (i + 1) * PAIR] for i in range(pairs)]

    @pl.loop(0, pairs)
    def _(p):
        qkv = dg(n1[...], wqkv[p], 1, 0)
        proj[p, :, 0:PAIR] = (qkv[:, 0:PAIR] + pick(p, q_bias)).astype(bf16)
        proj[p, :, PAIR : 2 * PAIR] = qkv[:, PAIR : 2 * PAIR].astype(bf16)
        proj[p, :, 2 * PAIR :] = (qkv[:, 2 * PAIR :] + pick(p, v_bias)).astype(bf16)

        def write(hh, o, total):
            ot[p, HD * hh : HD * hh + HD, :] = o.astype(bf16)
            lse[pl.ds(2 * p + hh, 1), :] = total

        attend(
            proj[p, :, PAIR : 2 * PAIR], proj[p, :, 2 * PAIR :].T,
            proj[p, :, 0:PAIR] * jnp.asarray(HD**-0.5, bf16), bias_k, write,
        )

    for p in range(pairs):
        att[:, p * PAIR : (p + 1) * PAIR] = ot[p].T
    send_out(proj, proj_hbm, sems.at[1])
    send_out(ot, ot_hbm, sems.at[2])
    send_out(lse, lse_hbm, sems.at[3])

    def branch(r, sl):
        a = att[sl, :]
        v = tok_ref[sl, :].astype(f32) + vec(PB)
        v += jnp.concatenate([dg(a, wproj[i], 1, 0) for i in range(2)], 1)
        res[sl, :] = v
        acc[sl, :] = v + vec(DB)
        gn2[sl, :] = jnp.zeros((rb, width), f32)
        n2[sl, :] = (norm_parts(v)[0] * vec(MG) + vec(MS)).astype(bf16)

    blocks(nb, rb, branch)
    n2t[...] = n2[...].T
    rm = 512
    staged = []
    for j in range(chunks):
        vg_ref[4 + j : 5 + j, :] = jnp.zeros((1, width), f32)

        def stage_one(r, sl, j=j):
            a, g = up_step(n2[sl, :], cot_ref[sl, :], lambda: wup[j], lambda: wdown[j], vec(UB + j))
            act[sl, :] = a
            gh[sl, :] = g
            acc[sl, :] += dg(a, wdown[j], 1, 0)
            gn2[sl, :] += dg(g, wup[j], 1, 1)
            vg_ref[4 + j : 5 + j, :] += jnp.sum(g.astype(f32), 0, keepdims=True)

        blocks(seq // rm, rm, stage_one)
        for cp in staged:
            cp.wait()
        gstage[0] = dg(act[...], cot_ref[...], 0, 0).astype(bf16)
        gstage[1] = dg(n2t[...], gh[...], 1, 0).astype(bf16)
        staged = [
            pltpu.make_async_copy(gstage.at[0], gdown_hbm.at[j], sems.at[4]),
            pltpu.make_async_copy(gstage.at[1], gup_hbm.at[j], sems.at[5]),
        ]
        for cp in staged:
            cp.start()

    vg_ref[0:4, :] = jnp.zeros((4, width), f32)

    def back_two(r, sl):
        n2[sl, :] = acc[sl, :].astype(bf16)
        g = gn2[sl, :]
        n, inv = norm_parts(res[sl, :])
        cot = cot_ref[sl, :].astype(f32)
        mid = cot + norm_back(n, inv, g * vec(MG))
        acc[sl, :] = mid
        low = mid.astype(bf16)
        act[sl, :] = low
        vg_ref[0:1, :] += jnp.sum(g * n, 0, keepdims=True)
        vg_ref[1:2, :] += jnp.sum(g, 0, keepdims=True)
        vg_ref[2:3, :] += jnp.sum(low.astype(f32), 0, keepdims=True)
        vg_ref[3:4, :] += jnp.sum(cot, 0, keepdims=True)
        gh[sl, :] = (dg(low[:, :half], wproj[0], 1, 1) + dg(low[:, half:], wproj[1], 1, 1)).astype(bf16)

    blocks(nb, rb, back_two)
    send_out(n2, out_hbm, sems.at[6])
    send_out(acc, gmid_hbm, sems.at[7])
    for p in range(pairs):
        send_out(gh.at[:, p * PAIR : (p + 1) * PAIR], do_hbm.at[p], sems.at[8 + p])
    for cp in staged:
        cp.wait()
    for i in range(2):
        gstage[i, :, :half] = dg(rows_of(ot[...]), act[:, i * half : (i + 1) * half], 1, 0).astype(bf16)
        send_out(gstage.at[i, :, pl.ds(0, half)], gproj_hbm.at[i], sems.at[4 + i])
    for cp in copies:
        cp.wait()


def backward_kernel(
    len_ref, tok_ref, vec_ref, proj_hbm, ot_hbm, lse_hbm, do_hbm, gmid_hbm, n1t_hbm, wqkv_ref,
    gin_hbm, gqkv_hbm, vg_ref,
    proj, ot, lse, do, gmid, n1t, gqkv, gin, sems,
):
    seq, width = tok_ref.shape
    pairs = proj.shape[0]

    def start(src, dst, sem):
        cp = pltpu.make_async_copy(src, dst, sem)
        cp.start()
        return cp

    loads = [
        start(proj_hbm, proj, sems.at[0]),
        start(do_hbm, do, sems.at[1]),
        start(ot_hbm, ot, sems.at[2]),
        start(lse_hbm, lse, sems.at[3]),
        start(n1t_hbm, n1t, sems.at[4]),
        start(gmid_hbm, gmid, sems.at[5]),
    ]
    for cp in loads:
        cp.wait()
    vg_ref[...] = jnp.zeros(vg_ref.shape, f32)
    bias_k = key_bias(len_ref[0], seq)

    @pl.loop(0, pairs)
    def _(p):
        dqt, dk, dv = attend_back(
            lambda sl: proj[p, sl, 0:PAIR],
            proj[p, :, PAIR : 2 * PAIR],
            proj[p, :, 2 * PAIR :],
            lambda sl: do[p, sl, :],
            lambda rows, sl: ot[p, rows, sl],
            lambda hh, sl: lse[pl.ds(2 * p + hh, 1), sl],
            bias_k,
            512,
            lambda: None,
        )
        proj[p, :, 0:PAIR] = dqt.T.astype(bf16)
        proj[p, :, PAIR : 2 * PAIR] = dk.astype(bf16)
        proj[p, :, 2 * PAIR :] = dv.astype(bf16)

    outs = []
    for p in range(pairs):
        cols = slice(p * PAIR, (p + 1) * PAIR)
        g = proj[p]
        sums = jnp.sum(g.astype(f32), 0, keepdims=True)
        vg_ref[2:3, cols] = sums[:, 0:PAIR]
        vg_ref[3:4, cols] = sums[:, 2 * PAIR :]
        gqkv[p] = dg(n1t[...], g, 1, 0).astype(bf16)
        outs.append(start(gqkv.at[p], gqkv_hbm.at[p], sems.at[6 + p]))

    def back_one(r, sl):
        g = dg(proj[0, sl, :], wqkv_ref[0], 1, 1)
        for p in range(1, pairs):
            g += dg(proj[p, sl, :], wqkv_ref[p], 1, 1)
        n, inv = norm_parts(tok_ref[sl, :].astype(f32))
        gin[sl, :] = (gmid[sl, :] + norm_back(n, inv, g * vec_ref[AG : AG + 1, :])).astype(bf16)
        vg_ref[0:1, :] += jnp.sum(g * n, 0, keepdims=True)
        vg_ref[1:2, :] += jnp.sum(g, 0, keepdims=True)

    blocks(seq // 256, 256, back_one)
    outs.append(start(gin, gin_hbm, sems.at[0]))
    for cp in outs:
        cp.wait()


def specs(kinds):
    table = {"s": pltpu.SMEM, "v": pltpu.VMEM, "h": pl.ANY}
    return [pl.BlockSpec(memory_space=table[k]) for k in kinds]


def sds(shape, dtype):
    return jax.ShapeDtypeStruct(shape, dtype)


def run_layer(nz, lengths, tokens, cotangent, vecs, wqkv, wproj, wup, wdown):
    seq, width = tokens.shape
    half = width // 2
    pairs = width // PAIR
    groups = pairs // 2
    own, rows = wup.shape[0], wdown.shape[0]
    piece = 32
    pieces = rows // piece
    sub = wup.shape[1] // pieces // 2
    chip = (2, nz, 2)
    padded = -(-own // 16) * 16

    def vmem(*dims, dtype=bf16):
        return pltpu.VMEM(dims, dtype)

    def landing(lead, block):
        return [pltpu.VMEM(lead + dims + block, bf16) for dims in (chip, (2, nz), (nz,), (nz - 1,))]

    qkv_landing = landing((groups,), (2 * own, 3 * PAIR))
    handover = [
        vmem(pieces, own, sub, dtype=f32),
        vmem(own, half, dtype=f32),
        vmem(groups, own, 3 * PAIR, dtype=f32),
    ]
    scratch = (
        [
            vmem(seq, width),
            vmem(width, seq),
            vmem(pairs, seq, 3 * PAIR),
            vmem(pairs, PAIR, seq),
            vmem(seq, width),
            vmem(2 * pairs, seq, dtype=f32),
            vmem(seq, width, dtype=f32),
            vmem(width, seq),
            vmem(seq, width, dtype=f32),
            vmem(seq, width, dtype=f32),
            vmem(seq, width),
            vmem(16, width, dtype=f32),
            vmem(pieces, 1, 2 * sub, dtype=f32),
            vmem(groups, 2, *chip, 2 * own, 3 * PAIR),
            vmem(2, *chip, 2 * own, half),
            vmem(pieces, 2, *chip, 2 * own, sub),
            vmem(pieces, *chip, 2, piece, width),
            vmem(*chip, 2, 16, PAIR),
            vmem(groups, padded, 3 * PAIR),
            vmem(padded, half),
            vmem(pieces, padded, sub),
            pltpu.SemaphoreType.DMA((5 + 2 * pieces, 8 + nz - 1)),
            pltpu.SemaphoreType.DMA((5 + 2 * pieces, 8 + nz - 1)),
            vmem(2, 5, 8, 2 * sub, dtype=f32),
        ]
        + landing((pieces,), (2 * own, sub))
        + landing((pieces,), (piece, width))
        + landing((), (2 * own, half))
        + qkv_landing[1:]
        + qkv_landing[:1]
        + handover
        + handover
        + [
            vmem(2, 2 + nz, 8, 2 * sub, dtype=f32),
            pltpu.SemaphoreType.DMA((12, 3 + nz)),
            pltpu.SemaphoreType.DMA((12, 3 + nz)),
            pltpu.SemaphoreType.DMA((12,)),
            pltpu.SemaphoreType.DMA((12,)),
            pltpu.SemaphoreType.DMA((2,)),
        ]
    )
    return pl.pallas_call(
        layer_kernel,
        in_specs=specs("shvvvvvv"),
        out_specs=specs("hhvvvvv"),
        out_shape=[
            sds((seq, width), bf16),
            sds((seq, width), bf16),
            sds((own, 3 * width), f32),
            sds((own, width), f32),
            sds((own, wup.shape[1]), f32),
            sds((rows, width), f32),
            sds((16, PAIR), f32),
        ],
        scratch_shapes=scratch,
        compiler_params=pltpu.CompilerParams(vmem_limit_bytes=VMEM_LIMIT, collective_id=0, has_side_effects=True),
        name="layer",
    )(lengths, tokens, cotangent, vecs, wqkv, wproj, wup, wdown)


def run_forward(lengths, tokens, cotangent, vecs, wqkv, wproj, wup, wdown):
    seq, width = tokens.shape
    pairs = width // PAIR
    chunks = wup.shape[0]
    return pl.pallas_call(
        forward_kernel,
        in_specs=specs("svvvvvvv"),
        out_specs=specs("hhhhhhhhhhv"),
        out_shape=[
            sds((seq, width), bf16),
            sds((pairs, seq, 3 * PAIR), bf16),
            sds((pairs, PAIR, seq), bf16),
            sds((2 * pairs, seq), f32),
            sds((pairs, seq, PAIR), bf16),
            sds((seq, width), f32),
            sds((width, seq), bf16),
            sds((chunks, width, width), bf16),
            sds((chunks, width, width), bf16),
            sds((2, width, width // 2), bf16),
            sds((8, width), f32),
        ],
        scratch_shapes=[
            pltpu.VMEM((seq, width), bf16),
            pltpu.VMEM((width, seq), bf16),
            pltpu.VMEM((pairs, seq, 3 * PAIR), bf16),
            pltpu.VMEM((pairs, PAIR, seq), bf16),
            pltpu.VMEM((seq, width), bf16),
            pltpu.VMEM((2 * pairs, seq), f32),
            pltpu.VMEM((seq, width), f32),
            pltpu.VMEM((seq, width), bf16),
            pltpu.VMEM((width, seq), bf16),
            pltpu.VMEM((seq, width), f32),
            pltpu.VMEM((seq, width), f32),
            pltpu.VMEM((seq, width), bf16),
            pltpu.VMEM((seq, width), bf16),
            pltpu.VMEM((2, width, width), bf16),
            pltpu.SemaphoreType.DMA((8 + pairs,)),
        ],
        compiler_params=pltpu.CompilerParams(vmem_limit_bytes=VMEM_LIMIT),
        name="layer_forward",
    )(lengths, tokens, cotangent, vecs, wqkv, wproj, wup, wdown)


def run_backward(lengths, tokens, vecs, proj, ot, lse, do, gmid, n1t, wqkv):
    seq, width = tokens.shape
    pairs = width // PAIR
    return pl.pallas_call(
        backward_kernel,
        in_specs=specs("svvhhhhhhv"),
        out_specs=specs("hhv"),
        out_shape=[
            sds((seq, width), bf16),
            sds((pairs, width, 3 * PAIR), bf16),
            sds((8, width), f32),
        ],
        scratch_shapes=[
            pltpu.VMEM((pairs, seq, 3 * PAIR), bf16),
            pltpu.VMEM((pairs, PAIR, seq), bf16),
            pltpu.VMEM((2 * pairs, seq), f32),
            pltpu.VMEM((pairs, seq, PAIR), bf16),
            pltpu.VMEM((seq, width), f32),
            pltpu.VMEM((width, seq), bf16),
            pltpu.VMEM((pairs, width, 3 * PAIR), bf16),
            pltpu.VMEM((seq, width), bf16),
            pltpu.SemaphoreType.DMA((6 + pairs,)),
        ],
        compiler_params=pltpu.CompilerParams(vmem_limit_bytes=VMEM_LIMIT),
        name="attention_backward",
    )(lengths, tokens, vecs, proj, ot, lse, do, gmid, n1t, wqkv)


def gathered(item, axis=0):
    return lax.all_gather(item, AXES, axis=axis, tiled=True)


def scattered(item, axis=0):
    return lax.psum_scatter(item, AXES, scatter_dimension=axis, tiled=True)


def per_device(
    nz, tokens, cotangent, lengths, attn_gain, attn_shift, qkv_weight, qv_bias, proj_weight, proj_bias,
    mlp_gain, mlp_shift, up_weight, up_bias, down_weight, down_bias,
):
    seq, width = tokens.shape
    pairs = width // PAIR
    own = attn_gain.shape[0]
    chunks = up_weight.shape[1] // width
    small = jnp.stack([attn_gain, attn_shift, qv_bias[0], qv_bias[1], proj_bias, mlp_gain, mlp_shift, down_bias])
    if nz:
        vecs = jnp.concatenate(
            [
                jnp.pad(small, ((0, 0), (0, PAIR - own))),
                jnp.pad(up_bias[None], ((0, 7), (0, PAIR - up_bias.shape[0]))),
            ]
        )
        block_out, input_grad, g_qkv, g_proj, g_up, g_down, v = run_layer(
            nz, lengths, tokens, cotangent, vecs, qkv_weight, proj_weight, up_weight, down_weight
        )
        w = v[:, :own]
        return (
            block_out, input_grad, w[8], w[9], g_qkv, w[10:12], g_proj, w[2], w[0], w[1],
            g_up, v[4:7, : up_bias.shape[0] // 3].reshape(-1), g_down, w[3],
        )
    allvec = gathered(jnp.concatenate([small.reshape(-1), up_bias])[None])
    many = allvec.shape[0]
    table = allvec[:, : 8 * own].reshape(many, 8, own).transpose(1, 0, 2).reshape(8, width)
    vecs = jnp.concatenate([table, allvec[:, 8 * own :].reshape(chunks, width)], 0).astype(f32)
    wqkv = gathered(qkv_weight).reshape(width, 3, pairs, PAIR).transpose(2, 0, 1, 3).reshape(pairs, width, 3 * PAIR)
    wproj = gathered(proj_weight).reshape(width, 2, width // 2).transpose(1, 0, 2)
    wup = gathered(up_weight).reshape(width, chunks, width).transpose(1, 0, 2)
    wdown = gathered(down_weight).reshape(chunks, width, width)
    block_out, proj, ot, lse, do, gmid, n1t, gup, gdown, gproj, vg_one = run_forward(
        lengths, tokens, cotangent, vecs, wqkv, wproj, wup, wdown
    )
    input_grad, gqkv, vg_two = run_backward(lengths, tokens, vecs, proj, ot, lse, do, gmid, n1t, wqkv)
    g_down = scattered(gdown.astype(f32).reshape(chunks * width, width))
    g_up = scattered(gup.astype(f32).transpose(1, 0, 2).reshape(width, chunks * width))
    g_proj = scattered(gproj.astype(f32).transpose(1, 0, 2).reshape(width, width))
    g_qkv = scattered(
        gqkv.astype(f32).reshape(pairs, width, 3, PAIR).transpose(1, 2, 0, 3).reshape(width, 3 * width)
    )
    rest = jnp.concatenate([vg_two[:4], vg_one[:4]], 0).reshape(8, many, own).transpose(1, 0, 2).reshape(many, -1)
    rest = jnp.concatenate([rest, vg_one[4:].reshape(many, -1)], 1)
    mine = scattered(rest)[0]
    v = mine[: 8 * own].reshape(8, own)
    return (
        block_out, input_grad, v[0], v[1], g_qkv, v[2:4], g_proj, v[6], v[4], v[5],
        g_up, mine[8 * own :], g_down, v[7],
    )


def chips_along_z(mesh):
    dp, shard = mesh.shape["dp"], mesh.shape["shard"]
    return shard // 4 if dp == 2 and shard == 16 else 0


def solution(mesh):
    one, two, mid = P(AXES), P(AXES, None), P(None, AXES)
    return jax.shard_map(
        functools.partial(per_device, chips_along_z(mesh)),
        mesh=mesh,
        in_specs=(two, two, one, one, one, two, mid, two, one, one, one, two, one, two, one),
        out_specs=(two, two, one, one, two, mid, two, one, one, one, two, one, two, one),
        check_vma=False,
    )
```

profile of v0, /device:TPU:0, one launch (start us, length us, event | category | flops | bytes accessed | tf_op | source)
XLA Modules:
  0.0 209.8 jit_solution(15168645968199316709)
XLA Ops:
  0.6 0.8 stack.28
  1.4 1.3 fusion.2.vec_in
  3.3 195.9 %layer.1 = (bf16[1024,768]{1,0:T(8,128)(2,1)}, bf16[1024,768]{1,0:T(8,128)(2,1)}, f32[24,2304]{1,0:T(8,128)}, f32[24,768]{1,0:T(8,128)}, f32[24,3072]{1,0:T(8,12...) custom-call(s32[1]{0:T(128)S(6)} %copy.35.len_ref, bf16[1024,768]{1,0:T(8,128)(2,1)} %tok_hbm.1, bf16[1024,768]{1,0:T(8,128)(2,1)} %cot_ref.1, ...), custom_call_target="tpu_custom_call" | custom-call | tf_op jit(solution)/shard_map/layer/pallas_call | solution.py:1082
  199.2 1.4 slice_bitcast_fusion
  200.6 0.7 slice.41
  201.3 0.6 reshape.31
  201.9 1.2 slice.37
  203.1 0.0 copy-start
  203.1 2.8 %copy.36 = bf16[1024,768]{1,0:T(8,128)(2,1)} copy(bf16[1024,768]{1,0:T(8,128)(2,1)} %get-tuple-element.48) | data formatting | bytes 3145728
  205.9 0.0 copy-done
  205.9 0.0 copy-start.3
  205.9 0.0 copy-start.4
  205.9 0.0 copy-start.2
  205.9 0.0 copy-start.1
  205.9 1.1 copy.37
  207.0 0.0 copy-done.3
  207.0 0.7 copy.38
  207.7 0.0 copy-done.4
  207.7 0.6 copy.39
  208.4 0.0 copy-done.2
  208.4 0.7 copy.40
  209.1 0.0 copy-done.1
  209.1 0.7 copy.41
Async XLA Ops:
  203.1 2.8 %copy-start = (bf16[1024,768]{1,0:T(8,128)(2,1)S(1)}, bf16[1024,768]{1,0:T(8,128)(2,1)}, u32[]{:S(2)}) copy-start(bf16[1024,768]{1,0:T(8,128)(2,1)} %get-tuple-element.49) | copy-start | bytes 4718596
  205.9 1.2 copy-start.3
  205.9 1.9 copy-start.4
  205.9 2.5 %copy-start.2 = (f32[24,3072]{1,0:T(8,128)S(1)}, f32[24,3072]{1,0:T(8,128)}, u32[]{:S(2)}) copy-start(f32[24,3072]{1,0:T(8,128)} %get-tuple-element.58) | copy-start | bytes 884740
  205.9 3.2 %copy-start.1 = (f32[96,768]{1,0:T(8,128)S(1)}, f32[96,768]{1,0:T(8,128)}, u32[]{:S(2)}) copy-start(f32[96,768]{1,0:T(8,128)} %get-tuple-element.60) | copy-start | bytes 884740
where the time goes:
time: 210 us
  Pallas kernels  196 us (93%)
  local copies, waits for them, and re-layouts  11.3 us (5%)
    pallas_call x1, Pallas kernels, run_layer(): pl.pallas_call(layer_kernel, in_specs=specs('shvvvvvv'), out_specs=specs(...  196 us
    unnamed x16, local copies, waits for them, and re-layouts  6.68 us

commit v1 on v0

--- a/solution.py
+++ b/solution.py
@@ -77,12 +77,15 @@
         return [self.peer(), self.a(), self.b()] + [self.along_z(k) for k in range(1, self.nz)]
 
 
-def enter(place):
-    barrier = pltpu.get_barrier_semaphore()
-    partners = place.partners()
-    for d in partners:
-        pl.semaphore_signal(barrier, inc=1, device_id=d, device_id_type=pl.DeviceIdType.MESH)
-    pl.semaphore_wait(barrier, len(partners))
+def greet(place):
+    for d in place.partners():
+        pl.semaphore_signal(
+            pltpu.get_barrier_semaphore(), inc=1, device_id=d, device_id_type=pl.DeviceIdType.MESH
+        )
+
+
+def met(place):
+    pl.semaphore_wait(pltpu.get_barrier_semaphore(), len(place.partners()))
 
 
 def remote(src, dst, send, recv, device):
@@ -303,7 +306,7 @@
     flat = vbuf[...].reshape(many * 16, PAIR)
 
     def spread(n, each, first=0):
-        lane = lax.broadcasted_iota(jnp.int32, (PAIR, n), 1)
+        lane = lax.broadcasted_iota(jnp.int32, (1, n), 1)
         row = lax.broadcasted_iota(jnp.int32, (PAIR, n), 0) - first
         return (lax.rem(lane, each) == row).astype(f32).astype(bf16)
 
@@ -329,7 +332,7 @@
 def regroup(pieces, piece):
     n = pieces * PAIR
     src = lax.broadcasted_iota(jnp.int32, (n, n), 0)
-    dst = lax.broadcasted_iota(jnp.int32, (n, n), 1)
+    dst = lax.broadcasted_iota(jnp.int32, (1, n), 1)
     inner = lax.rem(dst, PAIR)
     want = lax.div(inner, piece) * (pieces * piece) + lax.div(dst, PAIR) * piece + lax.rem(inner, piece)
     return (src == want).astype(f32)
@@ -377,10 +380,10 @@
     return items
 
 
-def slice_lanes(v, first, count):
+def slice_lanes(v, first, count, at=0):
     lane = lax.broadcasted_iota(jnp.int32, (v.shape[1], PAIR), 0) - first
-    out = lax.broadcasted_iota(jnp.int32, (v.shape[1], PAIR), 1)
-    pick = ((lane == out) & (out < count)).astype(f32)
+    out = lax.broadcasted_iota(jnp.int32, (v.shape[1], PAIR), 1) - at
+    pick = ((lane == out) & (out >= 0) & (out < count)).astype(f32)
     return lax.dot_general(
         v, pick, (((1,), (0,)), ((), ())), precision=lax.Precision.HIGHEST, preferred_element_type=f32
     )
@@ -450,41 +453,41 @@
 VECI, G0, G1, G2, PROJ, D0, U0, D1, U1, D2, U2 = range(11)
 SV1, SD0, SU0, SD1, SU1, SD2, SU2, SP, SG0, SG1, SG2, SV2 = range(20, 32)
 PLAN = {
-    "stats": [("B", VECI), ("B", G0), ("Z", G2), ("A", VECI), ("B", G1), ("A", G0), ("C", VECI), ("D", VECI)],
-    "norm": [("Z", PROJ), ("C", G0), ("B", G2), ("A", G1), ("Z", D0), ("D", G0)],
-    "f0": [("Z", U0), ("C", G1), ("A", G2), ("B", PROJ), ("B", D0)],
-    "f1": [("Z", D1), ("D", G1), ("C", G2), ("A", PROJ), ("B", U0)],
-    "f2": [("Z", U1), ("C", PROJ), ("A", D0), ("B", D1)],
-    "f3": [("Z", D2), ("D", G2), ("A", U0), ("B", U1), ("C", D0)],
-    "f4": [("Z", U2), ("A", D1), ("C", U0)],
-    "f5": [("B", D2), ("D", PROJ), ("D", D0), ("C", D1)],
-    "m0": [("D", U0), ("A", U1), ("B", U2)],
+    "stats": [("B", VECI), ("B", G0), ("Z", G2), ("A", VECI), ("B", G1), ("Z", PROJ), ("A", G0), ("C", VECI),
+              ("Z", D0), ("D", VECI), ("C", G0)],
+    "norm": [("A", G1), ("B", G2), ("Z", U0), ("D", G0)],
+    "f0": [("C", G1), ("A", G2), ("B", PROJ), ("B", D0), ("Z", D1)],
+    "f1": [("D", G1), ("C", G2), ("B", U0), ("Z", U1)],
+    "f2": [("A", PROJ), ("Z", D2)],
+    "f3": [("D", G2), ("A", D0), ("B", D1), ("Z", U2)],
+    "f4": [("A", U0), ("C", PROJ), ("B", U1)],
+    "f5": [("D", PROJ), ("C", D0)],
+    "m0": [("C", U0), ("A", D1), ("B", D2), ("D", D0), ("D", U0)],
     "m0g": [("finish", D0), ("finish", U0)],
-    "m1": [("A", D2), ("C", U1), ("D", D1)],
-    "m2": [("S0", SD0), ("S0", SU0), ("D", U1), ("A", U2), ("C", D2)],
+    "m1": [("A", U1), ("C", D1), ("B", U2)],
+    "m2": [("S0", SD0), ("S0", SU0), ("A", D2), ("C", U1), ("D", D1), ("D", U1)],
     "m2g": [("finish", D1), ("finish", U1)],
-    "m3": [("C", U2), ("D", D2), ("S1", SD0), ("S1", SU0)],
-    "m4": [("S0", SD1), ("S0", SU1), ("D", U2), ("S2", SD0)],
+    "m3": [("A", U2), ("C", D2), ("S1", SD0), ("S1", SU0)],
+    "m4": [("S0", SD1), ("S0", SU1), ("C", U2), ("S2", SD0), ("D", D2), ("D", U2)],
     "m4g": [("finish", D2), ("finish", U2)],
-    "m5": [("S1", SD1), ("S2", SU0)],
-    "m6": [("S0", SD2), ("S0", SU2), ("S1", SU1), ("S3", SD0), ("S2", SD1), ("finish", PROJ)],
-    "mid": [("S0", SP), ("S0", SV1), ("S1", SD2), ("S3", SU0), ("S4", SD0), ("S2", SU1)],
-    "b0h": [("S1", SU2), ("S3", SD1), ("S1", SV1)],
-    "b0": [("S1", SP), ("S2", SD2), ("S3", SU1), ("S4", SU0), ("S2", SV1)],
-    "b1h": [("S4", SD1), ("S5", SU0), ("S3", SV1)],
-    "b1": [("S0", SG0), ("S2", SU2), ("S4", SU1), ("S4", SV1)],
-    "b2h": [("S1", SG0), ("S2", SP), ("S3", SD2), ("S5", SU1), ("S3", SU2)],
-    "b2": [("S4", SD2)],
-    "b3h": [("S2", SG0), ("S3", SP), ("S4", SU2)],
-    "b3": [("S0", SG1), ("S3", SG0), ("S5", SU2), ("S4", SP)],
-    "b4h": [("S1", SG1), ("S5", SP)],
-    "b4": [("S4", SG0)],
-    "b5h": [("S2", SG1), ("S5", SG0)],
+    "m5": [("S2", SU0), ("S1", SD1)],
+    "m6": [("S0", SD2), ("S0", SU2), ("S3", SD0), ("S1", SU1), ("finish", PROJ)],
+    "mid": [("S0", SP), ("S0", SV1), ("S3", SU0), ("S2", SD1), ("S2", SU1), ("S1", SD2), ("S4", SD0)],
+    "b0h": [("S1", SV1), ("S1", SU2), ("S4", SU0)],
+    "b0": [("S2", SV1), ("S3", SD1), ("S3", SU1), ("S1", SP), ("S5", SU0)],
+    "b1h": [("S3", SV1), ("S2", SD2)],
+    "b1": [("S0", SG0), ("S2", SU2), ("S4", SD1), ("S4", SU1), ("S4", SV1)],
+    "b2h": [("S1", SG0), ("S2", SP), ("S5", SU1)],
+    "b2": [("S3", SD2)],
+    "b3h": [("S3", SU2), ("S2", SG0)],
+    "b3": [("S0", SG1), ("S3", SP), ("S3", SG0), ("S4", SD2)],
+    "b4h": [("S1", SG1), ("S4", SU2)],
+    "b4": [("S4", SP), ("S4", SG0), ("S5", SU2)],
+    "b5h": [("S2", SG1), ("S5", SP), ("S5", SG0)],
     "b5": [("S0", SG2), ("S3", SG1)],
     "r0": [("S1", SG2)],
-    "r1": [("S4", SG1)],
-    "r2": [("S5", SG1)],
-    "r3": [("S0", SV2), ("S2", SG2)],
+    "r2": [("S4", SG1)],
+    "r3": [("S0", SV2), ("S2", SG2), ("S5", SG1)],
     "end": [("S1", SV2), ("S3", SG2), ("S2", SV2), ("S3", SV2), ("S4", SG2), ("S4", SV2), ("S5", SG2)],
 }
 
@@ -616,6 +619,7 @@
 
     rb = 256
     nb = seq // rb
+    greet(place)
     tok_copy = pltpu.make_async_copy(tok_hbm, tok_early, sems.at[1])
     tok_copy.start()
     vbuf[p_.y, p_.z, p_.x, p_.c] = vec_in[...]
@@ -623,7 +627,7 @@
         for t in range(3):
             lanes = slice(t * width + p * PAIR, t * width + (p + 1) * PAIR)
             n2t[p * padded : p * padded + own, t * PAIR : (t + 1) * PAIR] = wqkv_in[:, lanes]
-    enter(place)
+    met(place)
     for i in (G0, G1, G2):
         items[i].X()
     items[VECI].Z()
@@ -696,7 +700,7 @@
     blocks(nb, rb, branch)
     n2t[...] = n2[...].T
 
-    rm = 512
+    rm = 1024
     @pl.loop(0, 2 * pieces)
     def _(turn):
         k, u = lax.div(turn, 2), lax.rem(turn, 2)
@@ -743,6 +747,7 @@
     blocks(nb, rb, back_two)
     out_copy = pltpu.make_async_copy(n2, out_hbm, sems.at[0])
     out_copy.start()
+    tok_again = pltpu.make_async_copy(tok_hbm, tok_late, sems.at[2])
     for i in range(2):
         v = dg(rows_of(ot[...]), act[:, i * half : (i + 1) * half], 1, 0).astype(bf16)
         wproj[i] = v.reshape(wproj.shape[1:])
@@ -775,6 +780,11 @@
         proj[p, :, PAIR : 2 * PAIR] = dk.astype(bf16)
         proj[p, :, 2 * PAIR :] = dv.astype(bf16)
 
+        @pl.when(p == 1)
+        def _():
+            out_copy.wait()
+            tok_again.start()
+
         @pl.when(lax.rem(p, 2) == 1)
         def _():
             g = lax.div(p, 2)
@@ -783,10 +793,7 @@
 
         ticks(p, [f"b{i}" for i in range(pairs)])
 
-    out_copy.wait()
-    tok_copy = pltpu.make_async_copy(tok_hbm, tok_late, sems.at[0])
-    tok_copy.start()
-    tok_copy.wait()
+    tok_again.wait()
 
     def back_one(r, sl):
         g = dg(proj[0, sl, :], rows_of(wqkv[0, 0]), 1, 1)
@@ -804,7 +811,7 @@
     index = ((p_.y * p_.nz + p_.z) * 2 + p_.x) * 2 + p_.c
     one = vsum[0, 4]
     vg_out[0:8, :] = slice_lanes(one, index * own, own)
-    vg_out[4:7, :] = slice_lanes(one, index * piece, piece)[4:7]
+    vg_out[4:5, :] = sum(slice_lanes(one, index * piece, piece, k * piece)[4 + k : 5 + k] for k in range(pieces))
     tick("end")
     vg_out[8:16, :] = slice_lanes(vsum[1, 4], index * own, own)
     for i, item in items.items():
@@ -1076,7 +1083,7 @@
             pltpu.SemaphoreType.DMA((12, 3 + nz)),
             pltpu.SemaphoreType.DMA((12,)),
             pltpu.SemaphoreType.DMA((12,)),
-            pltpu.SemaphoreType.DMA((2,)),
+            pltpu.SemaphoreType.DMA((3,)),
         ]
     )
     return pl.pallas_call(
@@ -1199,7 +1206,7 @@
         w = v[:, :own]
         return (
             block_out, input_grad, w[8], w[9], g_qkv, w[10:12], g_proj, w[2], w[0], w[1],
-            g_up, v[4:7, : up_bias.shape[0] // 3].reshape(-1), g_down, w[3],
+            g_up, v[4, : up_bias.shape[0]], g_down, w[3],
         )
     allvec = gathered(jnp.concatenate([small.reshape(-1), up_bias])[None])
     many = allvec.shape[0]

time: 210 us -> 203 us (0.967)
  Pallas kernels: 196 us -> 189 us
    pallas_call x1, Pallas kernels: 196 us -> 189 us  [run_layer(): pl.pallas_call(layer_kernel, in_specs=specs('shvvvvvv'), out_specs=specs(...]
where the time goes in v1:
time: 203 us
  Pallas kernels  189 us (93%)
  local copies, waits for them, and re-layouts  11.2 us (6%)
    pallas_call x1, Pallas kernels, run_layer(): pl.pallas_call(layer_kernel, in_specs=specs('shvvvvvv'), out_specs=specs(...  189 us
    unnamed x16, local copies, waits for them, and re-layouts  6.68 us

profile of v1, /device:TPU:0, one launch (start us, length us, event | category | flops | bytes accessed | tf_op | source)
XLA Modules:
  0.0 202.7 jit_solution(6549209639902874677)
XLA Ops:
  0.6 0.8 stack.28
  1.4 1.3 fusion.2.vec_in
  3.3 188.8 %layer.1 = (bf16[1024,768]{1,0:T(8,128)(2,1)}, bf16[1024,768]{1,0:T(8,128)(2,1)}, f32[24,2304]{1,0:T(8,128)}, f32[24,768]{1,0:T(8,128)}, f32[24,3072]{1,0:T(8,12...) custom-call(s32[1]{0:T(128)S(6)} %copy.35.len_ref, bf16[1024,768]{1,0:T(8,128)(2,1)} %tok_hbm.1, bf16[1024,768]{1,0:T(8,128)(2,1)} %cot_ref.1, ...), custom_call_target="tpu_custom_call" | custom-call | tf_op jit(solution)/shard_map/layer/pallas_call | solution.py:1089
  192.2 1.4 slice_bitcast_fusion
  193.6 1.2 slice.37
  194.8 1.2 slice_bitcast_fusion.1
  196.0 0.0 copy-start
  196.0 2.8 %copy.36 = bf16[1024,768]{1,0:T(8,128)(2,1)} copy(bf16[1024,768]{1,0:T(8,128)(2,1)} %get-tuple-element.48) | data formatting | bytes 3145728
  198.7 0.0 copy-done
  198.7 0.0 copy-start.3
  198.8 0.0 copy-start.4
  198.8 0.0 copy-start.2
  198.8 0.0 copy-start.1
  198.8 1.1 copy.37
  199.9 0.0 copy-done.3
  199.9 0.7 copy.38
  200.6 0.0 copy-done.4
  200.6 0.6 copy.39
  201.2 0.0 copy-done.2
  201.2 0.7 copy.40
  202.0 0.0 copy-done.1
  202.0 0.7 copy.41
Async XLA Ops:
  196.0 2.8 %copy-start = (bf16[1024,768]{1,0:T(8,128)(2,1)S(1)}, bf16[1024,768]{1,0:T(8,128)(2,1)}, u32[]{:S(2)}) copy-start(bf16[1024,768]{1,0:T(8,128)(2,1)} %get-tuple-element.49) | copy-start | bytes 4718596
  198.7 1.2 copy-start.3
  198.8 1.9 copy-start.4
  198.8 2.5 %copy-start.2 = (f32[24,3072]{1,0:T(8,128)S(1)}, f32[24,3072]{1,0:T(8,128)}, u32[]{:S(2)}) copy-start(f32[24,3072]{1,0:T(8,128)} %get-tuple-element.58) | copy-start | bytes 884740
  198.8 3.2 %copy-start.1 = (f32[96,768]{1,0:T(8,128)S(1)}, f32[96,768]{1,0:T(8,128)}, u32[]{:S(2)}) copy-start(f32[96,768]{1,0:T(8,128)} %get-tuple-element.60) | copy-start | bytes 884740

commit v2 on v1

--- a/solution.py
+++ b/solution.py
@@ -494,7 +494,7 @@
 
 def layer_kernel(
     len_ref, tok_hbm, cot_ref, vec_in, wqkv_in, wproj_in, wup_in, wdown_in,
-    out_hbm, gin_hbm, oqkv, oproj, oup, odown, vg_out,
+    out_hbm, gin_hbm, oqkv, oproj, oup, odown, vg_out, qv_out, ub_out,
     n1, n1t, proj, ot, att, lse, res, n2t, acc, gn2, gh,
     vec_ref, ub_ref, wqkv, wproj, wup, wdown, vbuf, xr_qkv, xr_proj, xr_up, gsend, grecv,
     vsum, up0, up1, up2, up3, down0, down1, down2, down3, proj0, proj1, proj2, proj3, qkv1, qkv2, qkv3,
@@ -811,9 +811,12 @@
     index = ((p_.y * p_.nz + p_.z) * 2 + p_.x) * 2 + p_.c
     one = vsum[0, 4]
     vg_out[0:8, :] = slice_lanes(one, index * own, own)
-    vg_out[4:5, :] = sum(slice_lanes(one, index * piece, piece, k * piece)[4 + k : 5 + k] for k in range(pieces))
+    up = sum(slice_lanes(one, index * piece, piece, k * piece)[4 + k : 5 + k] for k in range(pieces))
+    ub_out[...] = up[:, 0:rows]
     tick("end")
-    vg_out[8:16, :] = slice_lanes(vsum[1, 4], index * own, own)
+    late = slice_lanes(vsum[1, 4], index * own, own)
+    vg_out[8:16, :] = late
+    qv_out[...] = late[2:4, 0:own]
     for i, item in items.items():
         if i not in finished:
             item.finish()
@@ -1089,7 +1092,7 @@
     return pl.pallas_call(
         layer_kernel,
         in_specs=specs("shvvvvvv"),
-        out_specs=specs("hhvvvvv"),
+        out_specs=specs("hhvvvvvvv"),
         out_shape=[
             sds((seq, width), bf16),
             sds((seq, width), bf16),
@@ -1098,6 +1101,8 @@
             sds((own, wup.shape[1]), f32),
             sds((rows, width), f32),
             sds((16, PAIR), f32),
+            sds((2, own), f32),
+            sds((1, rows), f32),
         ],
         scratch_shapes=scratch,
         compiler_params=pltpu.CompilerParams(vmem_limit_bytes=VMEM_LIMIT, collective_id=0, has_side_effects=True),
@@ -1200,13 +1205,13 @@
                 jnp.pad(up_bias[None], ((0, 7), (0, PAIR - up_bias.shape[0]))),
             ]
         )
-        block_out, input_grad, g_qkv, g_proj, g_up, g_down, v = run_layer(
+        block_out, input_grad, g_qkv, g_proj, g_up, g_down, v, g_qv, g_ub = run_layer(
             nz, lengths, tokens, cotangent, vecs, qkv_weight, proj_weight, up_weight, down_weight
         )
         w = v[:, :own]
         return (
-            block_out, input_grad, w[8], w[9], g_qkv, w[10:12], g_proj, w[2], w[0], w[1],
-            g_up, v[4, : up_bias.shape[0]], g_down, w[3],
+            block_out, input_grad, w[8], w[9], g_qkv, g_qv, g_proj, w[2], w[0], w[1],
+            g_up, g_ub.reshape(-1), g_down, w[3],
         )
     allvec = gathered(jnp.concatenate([small.reshape(-1), up_bias])[None])
     many = allvec.shape[0]

time: 203 us -> 202 us (level)
    unnamed x16 -> x22, local copies, waits for them, and re-layouts: 6.68 us -> 7.76 us
where the time goes in v2:
time: 202 us
  Pallas kernels  189 us (94%)
  local copies, waits for them, and re-layouts  9.91 us (5%)
    pallas_call x1, Pallas kernels, run_layer(): pl.pallas_call(layer_kernel, in_specs=specs('shvvvvvv'), out_specs=specs(...  189 us
    unnamed x22, local copies, waits for them, and re-layouts  7.76 us

profile of v2, /device:TPU:0, one launch (start us, length us, event | category | flops | bytes accessed | tf_op | source)
XLA Modules:
  0.0 201.8 jit_solution(18375678127978431809)
XLA Ops:
  0.6 0.8 stack.28
  1.4 1.3 fusion.2.vec_in
  3.3 189.3 %layer.1 = (bf16[1024,768]{1,0:T(8,128)(2,1)}, bf16[1024,768]{1,0:T(8,128)(2,1)}, f32[24,2304]{1,0:T(8,128)}, f32[24,768]{1,0:T(8,128)}, f32[24,3072]{1,0:T(8,12...) custom-call(s32[1]{0:T(128)S(6)} %copy.37.len_ref, bf16[1024,768]{1,0:T(8,128)(2,1)} %tok_hbm.1, ...), custom_call_target="tpu_custom_call" | custom-call | tf_op jit(solution)/shard_map/layer/pallas_call | solution.py:1092
  192.7 1.4 slice_bitcast_fusion
  194.0 0.0 copy-start
  194.0 2.8 %copy.38 = bf16[1024,768]{1,0:T(8,128)(2,1)} copy(bf16[1024,768]{1,0:T(8,128)(2,1)} %get-tuple-element.52) | data formatting | bytes 3145728
  196.8 0.0 copy-done
  196.8 0.0 copy-start.3
  196.8 0.0 copy-start.2
  196.8 0.0 copy-start.6
  196.8 0.0 copy-start.1
  196.9 1.1 copy.39
  198.0 0.0 copy-done.3
  198.0 0.7 copy.40
  198.7 0.0 copy-done.5
  198.7 0.6 copy.41
  199.3 0.0 copy-done.4
  199.3 0.6 copy.42
  199.9 0.0 copy-done.2
  199.9 0.7 copy.43
  200.6 0.0 copy-done.6
  200.6 0.5 copy.44
  201.1 0.0 copy-done.1
  201.1 0.7 copy.45
  (2 shorter events, 0.0 us)
Async XLA Ops:
  194.0 2.8 %copy-start = (bf16[1024,768]{1,0:T(8,128)(2,1)S(1)}, bf16[1024,768]{1,0:T(8,128)(2,1)}, u32[]{:S(2)}) copy-start(bf16[1024,768]{1,0:T(8,128)(2,1)} %get-tuple-element.53) | copy-start | bytes 4718596
  196.8 1.2 copy-start.3
  196.8 1.9 copy-start.5
  196.8 2.4 %copy-start.4 = (f32[24,768]{1,0:T(8,128)S(1)}, f32[24,768]{1,0:T(8,128)}, u32[]{:S(2)}) copy-start(f32[24,768]{1,0:T(8,128)} %get-tuple-element.58) | copy-start | bytes 221188
  196.8 3.1 %copy-start.2 = (f32[24,3072]{1,0:T(8,128)S(1)}, f32[24,3072]{1,0:T(8,128)}, u32[]{:S(2)}) copy-start(f32[24,3072]{1,0:T(8,128)} %get-tuple-element.62) | copy-start | bytes 884740
  196.8 3.8 %copy-start.6 = (f32[1,96]{1,0:T(1,128)S(1)}, f32[1,96]{1,0:T(1,128)}, u32[]{:S(2)}) copy-start(f32[1,96]{1,0:T(1,128)} %get-tuple-element.30) | copy-start | bytes 1156
  196.8 4.3 %copy-start.1 = (f32[96,768]{1,0:T(8,128)S(1)}, f32[96,768]{1,0:T(8,128)}, u32[]{:S(2)}) copy-start(f32[96,768]{1,0:T(8,128)} %get-tuple-element.64) | copy-start | bytes 884740
